TPU v7x, 256 devices: a whole 4x4x8 slice. The times are simulated.
256 devices in a mesh: gx: 8 (over x, core), gy: 32 (over z, y).
Axes of the slice: x: 4, y: 4, z: 8, core: 2. Of those that a mesh axis runs over, the one named last changes fastest.
Arguments:
- multipoles: float32 [165, 524288], P(None, ('gx', 'gy')), may hold values from -6 to 6
- coarse_poles: float32 [165, 16384], P(None, ('gx', 'gy')), may hold values from -6 to 6
- operators: float32 [32, 165, 165], replicated, may hold values from -0.078125 to 0.078125
- block_lists: int32 [8192, 32], P(('gx', 'gy')), may hold values from -1 to 159, as said below
- coarse_lists: int32 [16384, 32], P(('gx', 'gy')), may hold values from -1 to 16383, as said below
- send_lists: int32 [256, 8, 16], P(('gx', 'gy')), may hold values from 0 to 143, as said below
- live_blocks: int32 [256], P(('gx', 'gy')), may hold values from 1 to 32
Outputs:
- fine_local: float32 [165, 524288], P(None, ('gx', 'gy'))
- coarse_local: float32 [165, 16384], P(None, ('gx', 'gy'))
Inputs may be any that keep to these rules, and one draw needn't show every extreme that they name: `send_lists`: at bit k, an entry indexes the 32 + k * 16 blocks held before that step. `block_lists`: -1 marks an empty slot. `coarse_lists`: -1 marks an empty slot.
All inputs are finite; a program needn't handle non-finite values.
Results may differ from a plain program's by a relative error of at most 0.0001.
Values sent between devices are 32-bit elements; how exact they have to be, the bound alone decides.
A program may use at most 192 MiB of HBM per device.

v0:
```python
import jax
import jax.numpy as jnp
from jax import lax
from jax.sharding import PartitionSpec as P

BCELLS = 64


def partner(shard, axis, bit):
    return lax.ppermute(shard, axis, [(i, i ^ 1 << bit) for i in range(lax.axis_size(axis))])


def coarse_terms(operators, everything, coarse_lists):
    coef_rows = everything.shape[1]
    count = everything.shape[0]
    extended = jnp.concatenate([everything, jnp.zeros((1, coef_rows), everything.dtype)], axis=0)
    safe = jnp.where(coarse_lists < 0, count, coarse_lists)
    taken = jnp.take(extended, safe.T.reshape(-1), axis=0).reshape(
        operators.shape[0], -1, coef_rows
    )
    return jnp.einsum(
        "jcd,jtd->ct",
        operators,
        taken,
        precision=lax.Precision.HIGHEST,
        preferred_element_type=jnp.float32,
    )


def shards(multipoles, coarse_poles, operators, block_lists, coarse_lists, send_lists, live_blocks):
    coef_rows = multipoles.shape[0]
    own_blocks = block_lists.shape[0]
    low_bits = lax.axis_size("gy").bit_length() - 1
    high_bits = lax.axis_size("gx").bit_length() - 1
    buffer = multipoles.reshape(coef_rows, own_blocks, BCELLS)
    for step in range(low_bits + high_bits):
        outgoing = jnp.take(buffer, send_lists[0, step], axis=1)
        if step < low_bits:
            incoming = partner(outgoing, "gy", step)
        else:
            incoming = partner(outgoing, "gx", step - low_bits)
        buffer = jnp.concatenate([buffer, incoming], axis=1)
    everything = lax.all_gather(coarse_poles.T, ("gx", "gy"), axis=0, tiled=True)
    extended = jnp.concatenate([buffer, jnp.zeros((coef_rows, 1, BCELLS), buffer.dtype)], axis=1)
    count = extended.shape[1]
    local = jnp.where(block_lists < 0, count - 1, block_lists)
    column_groups = local.T.reshape(-1, 8, own_blocks)
    operator_groups = operators.reshape(-1, 8, coef_rows, coef_rows)

    def group_step(total, pair):
        group_ops, columns = pair
        for inner in range(8):
            source = jnp.take(extended, columns[inner], axis=1).reshape(
                coef_rows, own_blocks * BCELLS
            )
            total = total + jnp.dot(
                group_ops[inner],
                source,
                precision=lax.Precision.HIGHEST,
                preferred_element_type=jnp.float32,
            )
        return (total, None)

    start = jnp.zeros((coef_rows, own_blocks * BCELLS), jnp.float32)
    fine_raw, _ = lax.scan(group_step, start, (operator_groups, column_groups))
    inside = jnp.arange(own_blocks, dtype=jnp.int32) < live_blocks[0]
    inside = jnp.repeat(inside, BCELLS)
    fine_local = jnp.where(inside[None, :], fine_raw, jnp.zeros_like(fine_raw))
    coarse_local = coarse_terms(operators, everything, coarse_lists)
    return (fine_local, coarse_local)


def solution(mesh):
    return jax.shard_map(
        shards,
        mesh=mesh,
        in_specs=(
            P(None, ("gx", "gy")),
            P(None, ("gx", "gy")),
            P(),
            P(("gx", "gy"), None),
            P(("gx", "gy"), None),
            P(("gx", "gy"), None, None),
            P(("gx", "gy")),
        ),
        out_specs=(P(None, ("gx", "gy")), P(None, ("gx", "gy"))),
        check_vma=False,
    )
```

profile of v0, /device:TPU:8, one launch (start us, length us, event | category | flops | bytes accessed | tf_op | source)
XLA Modules:
  0.0 724.6 jit_solution(13308554562794629814)
XLA Ops:
  14.1 22.7 %collective-permute-done = f32[165,16,64]{0,2,1:T(8,128)S(1)} collective-permute-done((f32[165,16,64]{0,2,1:T(8,128)S(1)}, f32[165,16,64]{0,2,1:T(8,128)S(1)}, u32[]{:S(2)}, u32[]{:S(2)}) %collective-permute-start) | collective-permute-done | bytes 675872 | tf_op jit(solution)/shard_map/ppermute | solution.py:10
  45.9 23.0 %collective-permute-done.1 = f32[165,16,64]{0,2,1:T(8,128)S(1)} collective-permute-done((f32[165,16,64]{0,2,1:T(8,128)S(1)}, f32[165,16,64]{0,2,1:T(8,128)S(1)}, u32[]{:S(2)}, u32[]{:S(2)}) %collective-permute-start.1) | collective-permute-done | bytes 675872 | tf_op jit(solution)/shard_map/ppermute | solution.py:10
  85.0 15.9 %collective-permute-done.2 = f32[165,16,64]{0,2,1:T(8,128)S(1)} collective-permute-done((f32[165,16,64]{0,2,1:T(8,128)S(1)}, f32[165,16,64]{0,2,1:T(8,128)S(1)}, u32[]{:S(2)}, u32[]{:S(2)}) %collective-permute-start.2) | collective-permute-done | bytes 675872 | tf_op jit(solution)/shard_map/ppermute | solution.py:10
  120.0 34.3 %collective-permute-done.3 = f32[165,16,64]{0,2,1:T(8,128)S(1)} collective-permute-done((f32[165,16,64]{0,2,1:T(8,128)S(1)}, f32[165,16,64]{0,2,1:T(8,128)S(1)}, u32[]{:S(2)}, u32[]{:S(2)}) %collective-permute-start.3) | collective-permute-done | bytes 675872 | tf_op jit(solution)/shard_map/ppermute | solution.py:10
  160.8 6.3 collective-permute-start.4
  167.1 45.7 %collective-permute-done.4 = f32[165,16,64]{0,2,1:T(8,128)S(1)} collective-permute-done((f32[165,16,64]{0,2,1:T(8,128)S(1)}, f32[165,16,64]{0,2,1:T(8,128)S(1)}, u32[]{:S(2)}, u32[]{:S(2)}) %collective-permute-start.4) | collective-permute-done | bytes 675872 | tf_op jit(solution)/shard_map/ppermute | solution.py:10
  228.2 16.6 %collective-permute-start.6 = (f32[165,16,64]{0,2,1:T(8,128)S(1)}, f32[165,16,64]{0,2,1:T(8,128)S(1)}, u32[]{:S(2)}, u32[]{:S(2)}) collective-permute-start(f32[165,16,64]{0,2,1:T(8,128)S(1)} %select_bitcast_fusion.1), channel_id=1, source_target_pairs={{0,64},{32,96},{64,0},{96,32},{128,192},{160,224},{192,128},{224,1... | collective-permute-start | bytes 2027528 | tf_op jit(solution)/shard_map/ppermute | solution.py:10
  244.8 8.0 %copy.12 = f32[32,165,165]{2,1,0:T(8,128)} copy(f32[32,165,165]{2,0,1:T(8,128)} %param.13) | data formatting | bytes 6969600 | tf_op args[2]
  254.5 14.6 %collective-permute-done.6 = f32[165,16,64]{0,2,1:T(8,128)S(1)} collective-permute-done((f32[165,16,64]{0,2,1:T(8,128)S(1)}, f32[165,16,64]{0,2,1:T(8,128)S(1)}, u32[]{:S(2)}, u32[]{:S(2)}) %collective-permute-start.6) | collective-permute-done | bytes 675872 | tf_op jit(solution)/shard_map/ppermute | solution.py:10
  279.5 21.5 %collective-permute-done.7 = f32[165,16,64]{0,2,1:T(8,128)S(1)} collective-permute-done((f32[165,16,64]{0,2,1:T(8,128)S(1)}, f32[165,16,64]{0,2,1:T(8,128)S(1)}, u32[]{:S(2)}, u32[]{:S(2)}) %collective-permute-start.7) | collective-permute-done | bytes 675872 | tf_op jit(solution)/shard_map/ppermute | solution.py:10
  302.8 378.3 %while.11 = (s32[]{:T(128)}, f32[165,2048]{1,0:T(8,128)S(1)}, f32[4,8,165,165]{3,2,1,0:T(8,128)}, s32[4,8,32]{2,1,0:T(8,128)S(1)}, f32[165,161,64]{0,2,1:T(8,128...) while((s32[]{:T(128)}, f32[165,2048]{1,0:T(8,128)S(1)}, ...), condition=%wide.region_1.3_spmd.clone, body=%wide.region_0.0_spmd.clone.sunk | while | flops 5358407168 | bytes 101821288 | solution.py:65
  307.5 6.0 gather_fusion.1
  331.1 6.0 gather_fusion.3
  355.3 6.4 gather_fusion.5
  379.5 6.4 gather_fusion.7
  403.5 6.0 gather_fusion.1
  427.0 6.0 gather_fusion.3
  450.5 6.0 gather_fusion.5
  474.0 6.0 gather_fusion.7
  497.5 6.0 gather_fusion.1
  521.0 6.0 gather_fusion.3
  682.9 11.3 %concatenate.42 = f32[16385,165]{1,0:T(8,128)} pad(f32[16384,165]{1,0:T(8,128)} %all-gather.2.cloned.1.call-done, f32[]{:T(128)} %constant.114.clone.1), padding=0_1x0_0 | pad | bytes 21627544 | tf_op jit(solution)/shard_map/concatenate | solution.py:16
  694.3 12.4 %gather_fusion.16 = f32[2048,165]{1,0:T(8,128)S(1)} fusion(f32[16385,165]{1,0:T(8,128)} %concatenate.42, s32[2048]{0:T(1024)S(1)} %copy-done.10), kind=kCustom, calls=%fused_computation.16 | custom fusion | bytes 2711552 | tf_op jit(solution)/shard_map/jit(_take)/gather | solution.py:18
  706.7 10.7 %fusion.10 = f32[165,64]{0,1:T(8,128)} fusion(f32[32,64,165]{2,1,0:T(8,128)S(1)} %bitcast.224, pred[32,64]{1,0:T(8,128)(4,1)S(1)} %copy-done.11, f32[32,165,165]{2,0,1:T(8,128)} %param.13), kind=kOutput, calls=%fused_computation.79 | convolution fusion | flops 669419520 | bytes 4880768 | tf_op jit(solution)/shard_map/jcd,jtd->ct/dot_general | solution.py:21
  (222 shorter events, 404.5 us)
Async XLA Ops:
  7.2 675.8 %all-gather.2.cloned.1.call-start = ((), (), s32[]{:S(2)}) async-start(), calls=%async_computation | async-start | bytes 16842752 | tf_op jit(solution)/shard_map/all_gather | solution.py:43
  11.8 25.0 %collective-permute-start = (f32[165,16,64]{0,2,1:T(8,128)S(1)}, f32[165,16,64]{0,2,1:T(8,128)S(1)}, u32[]{:S(2)}, u32[]{:S(2)}) collective-permute-start(f32[165,16,64]{0,2,1:T(8,128)S(1)} %select_bitcast_fusion.7), channel_id=1, source_target_pairs={{0,1},{1,0},{2,3},{3,2},{4,5},{5,4},{6,7},{7,6},{8,9},{9,8},{10,11... | collective-permute-start | bytes 2027528 | tf_op jit(solution)/shard_map/ppermute | solution.py:10
  43.5 25.4 %collective-permute-start.1 = (f32[165,16,64]{0,2,1:T(8,128)S(1)}, f32[165,16,64]{0,2,1:T(8,128)S(1)}, u32[]{:S(2)}, u32[]{:S(2)}) collective-permute-start(f32[165,16,64]{0,2,1:T(8,128)S(1)} %select_bitcast_fusion.6), channel_id=1, source_target_pairs={{0,2},{1,3},{2,0},{3,1},{4,6},{5,7},{6,4},{7,5},{8,10},{9,11},{10,... | collective-permute-start | bytes 2027528 | tf_op jit(solution)/shard_map/ppermute | solution.py:10
  77.4 23.6 %collective-permute-start.2 = (f32[165,16,64]{0,2,1:T(8,128)S(1)}, f32[165,16,64]{0,2,1:T(8,128)S(1)}, u32[]{:S(2)}, u32[]{:S(2)}) collective-permute-start(f32[165,16,64]{0,2,1:T(8,128)S(1)} %select_bitcast_fusion.5), channel_id=1, source_target_pairs={{0,4},{1,5},{2,6},{3,7},{4,0},{5,1},{6,2},{7,3},{8,12},{9,13},{10,... | collective-permute-start | bytes 2027528 | tf_op jit(solution)/shard_map/ppermute | solution.py:10
  79.6 22.3 %copy-start.5 = (f32[165,16,64]{0,2,1:T(8,128)S(1)}, f32[165,16,64]{0,2,1:T(8,128)}, u32[]{:S(2)}) copy-start(f32[165,16,64]{0,2,1:T(8,128)} %copy-done.4) | copy-start | bytes 2027524
  107.9 46.4 %collective-permute-start.3 = (f32[165,16,64]{0,2,1:T(8,128)S(1)}, f32[165,16,64]{0,2,1:T(8,128)S(1)}, u32[]{:S(2)}, u32[]{:S(2)}) collective-permute-start(f32[165,16,64]{0,2,1:T(8,128)S(1)} %select_bitcast_fusion.4), channel_id=1, source_target_pairs={{0,8},{1,9},{2,10},{3,11},{4,12},{5,13},{6,14},{7,15},{8,0},{9,1},... | collective-permute-start | bytes 2027528 | tf_op jit(solution)/shard_map/ppermute | solution.py:10
  160.8 52.0 %collective-permute-start.4 = (f32[165,16,64]{0,2,1:T(8,128)S(1)}, f32[165,16,64]{0,2,1:T(8,128)S(1)}, u32[]{:S(2)}, u32[]{:S(2)}) collective-permute-start(f32[165,16,64]{0,2,1:T(8,128)S(1)} %select_bitcast_fusion.3), channel_id=1, source_target_pairs={{0,16},{1,17},{2,18},{3,19},{4,20},{5,21},{6,22},{7,23},{8,24},{9,... | collective-permute-start | bytes 2027528 | tf_op jit(solution)/shard_map/ppermute | solution.py:10
  219.2 2.7 collective-permute-start.5
  228.2 40.9 %collective-permute-start.6 = (f32[165,16,64]{0,2,1:T(8,128)S(1)}, f32[165,16,64]{0,2,1:T(8,128)S(1)}, u32[]{:S(2)}, u32[]{:S(2)}) collective-permute-start(f32[165,16,64]{0,2,1:T(8,128)S(1)} %select_bitcast_fusion.1), channel_id=1, source_target_pairs={{0,64},{32,96},{64,0},{96,32},{128,192},{160,224},{192,128},{224,1... | collective-permute-start | bytes 2027528 | tf_op jit(solution)/shard_map/ppermute | solution.py:10
  244.8 8.1 %copy-start.12 = (s32[32,32]{1,0:T(8,128)S(1)}, s32[32,32]{1,0:T(8,128)}, u32[]{:S(2)}) copy-start(s32[32,32]{1,0:T(8,128)} %param.14) | copy-start | bytes 12292
  244.8 9.5 %copy-start.9 = (s32[64,32]{0,1:T(8,128)S(1)}, s32[64,32]{0,1:T(8,128)}, u32[]{:S(2)}) copy-start(s32[64,32]{0,1:T(8,128)} %param.15) | copy-start | bytes 24580
  275.1 25.9 %collective-permute-start.7 = (f32[165,16,64]{0,2,1:T(8,128)S(1)}, f32[165,16,64]{0,2,1:T(8,128)S(1)}, u32[]{:S(2)}, u32[]{:S(2)}) collective-permute-start(f32[165,16,64]{0,2,1:T(8,128)S(1)} %select_bitcast_fusion), channel_id=1, source_target_pairs={{0,128},{32,160},{64,192},{96,224},{128,0},{160,32},{192,64},{224,... | collective-permute-start | bytes 2027528 | tf_op jit(solution)/shard_map/ppermute | solution.py:10
  317.5 5.2 copy-start.3
  341.1 5.1 copy-start.1
  365.7 5.2 copy-start.2
  389.9 5.1 copy-start
  413.4 5.1 copy-start.3
  460.4 5.1 copy-start.2
  507.5 5.1 copy-start.3
  554.5 5.1 copy-start.2
  601.6 5.1 copy-start.3
  648.6 5.1 copy-start.2
  682.9 11.3 %copy-start.10 = (s32[2048]{0:T(1024)S(1)}, s32[2048]{0:T(1024)}, u32[]{:S(2)}) copy-start(s32[2048]{0:T(1024)} %broadcast_clamp_fusion) | copy-start | bytes 24580
  694.3 12.4 %copy-start.11 = (pred[32,64]{1,0:T(8,128)(4,1)S(1)}, pred[32,64]{1,0:T(8,128)(4,1)}, u32[]{:S(2)}) copy-start(pred[32,64]{1,0:T(8,128)(4,1)} %compare_and_fusion.8) | copy-start | bytes 6148
  (10 other events, 38.7 us)
Sparse Core Ops, SparseCore 0:
  244.9 137.6 all-gather.1
where the time goes:
time: 734 us; the launch traced here: 725 us
  local copies, waits for them, and re-layouts  261 us (36%)
  waiting for transfers between devices  181 us (25%)
  matrix products  152 us (21%)
  other arithmetic  79.1 us (11%)
  starting transfers between devices  36.4 us (5%)
  between operations  15.3 us (2%)
    ppermute x8, waiting for transfers between devices, partner(): lax.ppermute(shard, axis, [(i, i ^ 1 << bit) for i in range(lax.axis_size...  180 us
    gather x32, local copies, waits for them, and re-layouts, group_step(): jnp.take(extended, columns[inner], axis=1)  173 us
    dot_general x32, matrix products, group_step(): jnp.dot(group_ops[inner], source, precision=lax.Precision.HIGHEST, prefer...  141 us
    select_n x16, other arithmetic, group_step(): jnp.take(extended, columns[inner], axis=1)  63.3 us
    ppermute x8, starting transfers between devices, partner(): lax.ppermute(shard, axis, [(i, i ^ 1 << bit) for i in range(lax.axis_size...  36.3 us
    unnamed x28, local copies, waits for them, and re-layouts  34.6 us
    gather x8, local copies, waits for them, and re-layouts, shards(): outgoing = jnp.take(buffer, send_lists[0, step], axis=1)  26.4 us
  transfers between devices with their start and end apart: 9, of which 8 were waited for; matrix products, arithmetic and copies ran while one was open for 57% of the time, Pallas kernels for 0%

commit v1 on v0

v1 whole, which is shorter than its diff:
```python
import functools
import jax
import jax.numpy as jnp
from jax import lax
from jax.experimental import pallas as pl
from jax.experimental.pallas import tpu as pltpu
from jax.sharding import PartitionSpec as P

BCELLS = 64
ROWS = 16
MESH = pl.DeviceIdType.MESH


def coarse_terms(operators, everything, coarse_lists):
    coef_rows = everything.shape[1]
    count = everything.shape[0]
    extended = jnp.concatenate([everything, jnp.zeros((1, coef_rows), everything.dtype)], axis=0)
    safe = jnp.where(coarse_lists < 0, count, coarse_lists)
    taken = jnp.take(extended, safe.T.reshape(-1), axis=0).reshape(
        operators.shape[0], -1, coef_rows
    )
    return jnp.einsum(
        "jcd,jtd->ct",
        operators,
        taken,
        precision=lax.Precision.HIGH,
        preferred_element_type=jnp.float32,
    )


def lanes_below(shape, limit):
    return lax.broadcasted_iota(jnp.int32, shape, len(shape) - 1) < limit


def fine_kernel(
    groups, steps, own, sent, low_bits, offsets,
    mult_ref, ops_ref, send_ref, lists_ref, live_ref,
    out_ref,
    table, outgo, landed, split, mats, total, send_sem, recv_sem,
):
    slots, coef, _ = ops_ref.shape
    gx = lax.axis_index("gx")
    gy = lax.axis_index("gy")

    def partner(k):
        if k < low_bits:
            bit = 1 << k
            up = lax.rem(gy // bit, 2)
            return (gx, gy + bit - 2 * bit * up)
        bit = 1 << (k - low_bits)
        up = lax.rem(gx // bit, 2)
        return (gx + bit - 2 * bit * up, gy)

    def copy(g, k):
        return pltpu.make_async_remote_copy(
            src_ref=outgo.at[g, k],
            dst_ref=landed.at[g, k],
            send_sem=send_sem.at[g, k],
            recv_sem=recv_sem.at[g, k],
            device_id=partner(k),
            device_id_type=MESH,
        )

    barrier = pltpu.get_barrier_semaphore()
    for k in range(steps):
        pl.semaphore_signal(barrier, inc=1, device_id=partner(k), device_id_type=MESH)

    half = lanes_below((8, 128), 64)

    def own_blocks(g, carry):
        def pair(p, c):
            lanes = pl.ds(pl.multiple_of(p * 128, 128), 128)
            first = mult_ref[pl.ds(pl.multiple_of(g * ROWS, 8), 8), lanes]
            second = mult_ref[pl.ds(pl.multiple_of(g * ROWS + 8, 8), 8), lanes]
            table[g, 2 * p] = jnp.where(half, first, pltpu.roll(second, 64, 1))
            table[g, 2 * p + 1] = jnp.where(half, pltpu.roll(first, 64, 1), second)
            return c

        return lax.fori_loop(0, own // 2, pair, carry, unroll=True)

    lax.fori_loop(0, groups, own_blocks, 0)
    split[0] = jnp.zeros((ROWS, 128), jnp.bfloat16)
    pl.semaphore_wait(barrier, steps)

    def send(g, k):
        if k > 0:
            copy(g, k - 1).wait_recv()
            first = own + (k - 1) * sent
            table[g, first : first + sent] = landed[g, k - 1]
        for i in range(sent):
            outgo[g, k, i] = table[g, send_ref[k, i]]
        copy(g, k).start()

    def arrange(q):
        per = 128 // ROWS
        lane = lax.broadcasted_iota(jnp.int32, (ROWS, 128), 1)
        tail = coef - 128

        def rows_at(read, at):
            tiles = []
            for i in range(per):
                full = read(q * per + i)
                tiles.append(
                    (
                        full[:, :128],
                        jnp.concatenate(
                            [full[:, 128:], jnp.zeros((ROWS, 128 - tail), jnp.float32)], axis=1
                        ),
                    )
                )
            for g in range(groups):
                which, at_lane = divmod(g * ROWS, 128)
                value = jnp.zeros((ROWS, 128), jnp.float32)
                for i in range(per):
                    shift = (i * ROWS - at_lane) % 128
                    piece = tiles[i][which]
                    if shift:
                        piece = pltpu.roll(piece, shift, 1)
                    value = jnp.where((lane >= i * ROWS) & (lane < (i + 1) * ROWS), piece, value)
                high = value.astype(jnp.bfloat16)
                low = (value - high.astype(jnp.float32)).astype(jnp.bfloat16)
                height = mats.shape[1] // 2
                mats[g, pl.ds(at, ROWS), pl.ds(pl.multiple_of(q * 128, 128), 128)] = high
                mats[g, pl.ds(height + at, ROWS), pl.ds(pl.multiple_of(q * 128, 128), 128)] = low

        whole = coef // ROWS

        def body(r, c):
            at = pl.multiple_of(r * ROWS, ROWS)
            rows_at(lambda j: ops_ref[j, pl.ds(at, ROWS), :], at)
            return c

        lax.fori_loop(0, whole, body, 0)
        left = coef - whole * ROWS
        rows_at(
            lambda j: jnp.concatenate(
                [
                    ops_ref[j, whole * ROWS : coef, :],
                    jnp.zeros((ROWS - left, coef), jnp.float32),
                ],
                axis=0,
            ),
            whole * ROWS,
        )

    def multiply(g):
        copy(g, steps - 1).wait_recv()
        first = own + (steps - 1) * sent
        table[g, first : first + sent] = landed[g, steps - 1]
        halves = lanes_below((16, 8, 128), 64)

        def cut(c, carry):
            at = pl.multiple_of(c * 16, 16)
            block = table[g, pl.ds(at, 16)]
            high = block.astype(jnp.bfloat16).astype(jnp.float32)
            low = block - high
            top = jnp.where(halves, high, pltpu.roll(low, 64, 2))
            bottom = jnp.where(halves, pltpu.roll(high, 64, 2), low)
            split[pl.ds(at + 1, 16)] = jnp.concatenate([top, bottom], axis=1).astype(jnp.bfloat16)
            return carry

        lax.fori_loop(0, (own + steps * sent) // 16, cut, 0)
        height = mats.shape[1] // 2

        def targets(p, carry):
            sides = []
            for side in range(2):
                sides.append(
                    jnp.concatenate(
                        [split[lists_ref[2 * p + side, j] + 1] for j in range(slots)], axis=0
                    )
                )
            source = jnp.concatenate(sides, axis=1)
            product = jnp.dot(mats[g], source, preferred_element_type=jnp.float32)
            lanes = pl.ds(pl.multiple_of(p * 256, 256), 256)
            total[:, lanes] += product[:height] + product[height:]
            return carry

        lax.fori_loop(0, own // 2, targets, 0)

    total[...] = jnp.zeros_like(total)

    def tick(s, carry):
        for k in reversed(range(steps)):
            g = s - offsets[k]

            @pl.when((g >= 0) & (g < groups))
            def _():
                send(g, k)

        @pl.when(s < slots * ROWS // 128)
        def _():
            arrange(s)

        g = s - offsets[steps]

        @pl.when((g >= 0) & (g < groups))
        def _():
            multiply(g)

        return carry

    lax.fori_loop(0, groups + offsets[steps], tick, 0)

    def drain(g, carry):
        for k in range(steps):
            copy(g, k).wait_send()
        return carry

    lax.fori_loop(0, groups, drain, 0)

    live = live_ref[0]
    side = lanes_below((coef, 128), 64)

    def finish(p, carry):
        left = total[:coef, pl.ds(pl.multiple_of(p * 256, 256), 128)]
        right = total[:coef, pl.ds(pl.multiple_of(p * 256 + 128, 128), 128)]
        left = left + pltpu.roll(left, 64, 1)
        right = right + pltpu.roll(right, 64, 1)
        both = jnp.where(side, left, right)
        position = 2 * p + jnp.where(side, 0, 1)
        out_ref[:, pl.ds(pl.multiple_of(p * 128, 128), 128)] = jnp.where(position < live, both, 0.0)
        return carry

    lax.fori_loop(0, own // 2, finish, 0)


def fine_part(multipoles, operators, block_lists, send_lists, live_blocks):
    coef, cells = multipoles.shape
    slots = operators.shape[0]
    own = cells // BCELLS
    _, steps, sent = send_lists.shape
    groups = -(-coef // ROWS)
    low_bits = lax.axis_size("gy").bit_length() - 1
    offsets = tuple(range(steps + 1))
    padded = jnp.pad(multipoles, ((0, groups * ROWS - coef), (0, 0)))
    vmem = pl.BlockSpec(memory_space=pltpu.VMEM)
    smem = pl.BlockSpec(memory_space=pltpu.SMEM)
    return pl.pallas_call(
        functools.partial(fine_kernel, groups, steps, own, sent, low_bits, offsets),
        out_shape=jax.ShapeDtypeStruct((coef, cells), jnp.float32),
        in_specs=[vmem, vmem, smem, smem, smem],
        out_specs=vmem,
        scratch_shapes=[
            pltpu.VMEM((groups, own + steps * sent, 8, 128), jnp.float32),
            pltpu.VMEM((groups, steps, sent, 8, 128), jnp.float32),
            pltpu.VMEM((groups, steps, sent, 8, 128), jnp.float32),
            pltpu.VMEM((own + steps * sent + 1, ROWS, 128), jnp.bfloat16),
            pltpu.VMEM((groups, 2 * groups * ROWS, slots * ROWS), jnp.bfloat16),
            pltpu.VMEM((groups * ROWS, own * 128), jnp.float32),
            pltpu.SemaphoreType.DMA((groups, steps)),
            pltpu.SemaphoreType.DMA((groups, steps)),
        ],
        compiler_params=pltpu.CompilerParams(
            collective_id=0, has_side_effects=True, vmem_limit_bytes=60 << 20
        ),
        cost_estimate=pl.CostEstimate(
            flops=8 * slots * coef * coef * cells, bytes_accessed=8 << 20, transcendentals=0
        ),
        name="fine",
    )(padded, operators, send_lists[0], block_lists, live_blocks)


def shards(multipoles, coarse_poles, operators, block_lists, coarse_lists, send_lists, live_blocks):
    everything = lax.all_gather(coarse_poles.T, ("gx", "gy"), axis=0, tiled=True)
    fine_local = fine_part(multipoles, operators, block_lists, send_lists, live_blocks)
    coarse_local = coarse_terms(operators, everything, coarse_lists)
    return (fine_local, coarse_local)


def solution(mesh):
    return jax.shard_map(
        shards,
        mesh=mesh,
        in_specs=(
            P(None, ("gx", "gy")),
            P(None, ("gx", "gy")),
            P(),
            P(("gx", "gy"), None),
            P(("gx", "gy"), None),
            P(("gx", "gy"), None, None),
            P(("gx", "gy")),
        ),
        out_specs=(P(None, ("gx", "gy")), P(None, ("gx", "gy"))),
        check_vma=False,
    )
```

time: 734 us -> 211 us (0.29)
  local copies, waits for them, and re-layouts: 261 us -> 34.4 us
  waiting for transfers between devices: 181 us -> 0.7 us
  Pallas kernels: 0 us -> 149 us
  matrix products: 152 us -> 9.05 us
  other arithmetic: 79.1 us -> 0.75 us
  starting transfers between devices: 36.4 us -> 0.04 us
    gather x40 -> x0, local copies, waits for them, and re-layouts: 199 us -> none  [the longest x32 173 us: group_step(): jnp.take(extended, columns[inner], axis=1)]
    ppermute x8 -> x0, waiting for transfers between devices: 180 us -> none  [partner(): lax.ppermute(shard, axis, [(i, i ^ 1 << bit) for i in range(lax.axis_size...]
    pallas_call x0 -> x1, Pallas kernels: none -> 149 us  [fine_part(): pl.pallas_call(functools.partial(fine_kernel, groups, steps, own, sent, l...]
    dot_general x33 -> x1, matrix products: 152 us -> 9.05 us  [coarse_terms(): jnp.einsum('jcd,jtd->ct', operators, taken, precision=lax.Precision.HIGH,...]
    select_n x26 -> x0, other arithmetic: 69.6 us -> none  [the longest x16 63.3 us: group_step(): jnp.take(extended, columns[inner], axis=1)]
    ppermute x8 -> x0, starting transfers between devices: 36.3 us -> none  [partner(): lax.ppermute(shard, axis, [(i, i ^ 1 << bit) for i in range(lax.axis_size...]
    unnamed x28 -> x8, local copies, waits for them, and re-layouts: 34.6 us -> 9.26 us
  transfers between devices with their start and end apart: 9 -> 1, of which waited for: 8 -> 0; matrix products, arithmetic and copies ran while one was open for 57% -> 5% of each run, Pallas kernels for 0% -> 71%
where the time goes in v1:
time: 211 us; the launch traced here: 208 us
  Pallas kernels  149 us (71%)
  local copies, waits for them, and re-layouts  34.4 us (16%)
  between operations  14.8 us (7%)
  matrix products  9.05 us (4%)
    pallas_call x1, Pallas kernels, fine_part(): pl.pallas_call(functools.partial(fine_kernel, groups, steps, own, sent, l...  149 us
    gather x1, local copies, waits for them, and re-layouts, coarse_terms(): jnp.take(extended, safe.T.reshape(-1), axis=0)  12.4 us
    concatenate x1, local copies, waits for them, and re-layouts, coarse_terms(): jnp.concatenate([everything, jnp.zeros((1, coef_rows), everything.dtype)]...  11.4 us
    unnamed x8, local copies, waits for them, and re-layouts  9.26 us
    dot_general x1, matrix products, coarse_terms(): jnp.einsum('jcd,jtd->ct', operators, taken, precision=lax.Precision.HIGH,...  9.05 us
  transfers between devices with their start and end apart: 1, of which 0 were waited for; matrix products, arithmetic and copies ran while one was open for 5% of the time, Pallas kernels for 71%

profile of v1, /device:TPU:8, one launch (start us, length us, event | category | flops | bytes accessed | tf_op | source)
XLA Modules:
  0.0 208.4 jit_solution(1727526093337159159)
XLA Ops:
  7.2 0.0 all-gather.2.cloned.1.call-start
  7.2 0.7 all-gather.2.cloned.1.call-update
  7.9 0.7 fusion.7
  8.6 0.1 reshape.47
  8.7 0.0 copy-start
  8.7 8.2 %copy.9.ops_ref = f32[32,165,165]{2,1,0:T(8,128)} copy(f32[32,165,165]{2,0,1:T(8,128)} %param.9) | data formatting | bytes 6969600 | tf_op args[2]
  17.5 0.0 copy-done
  17.5 1.3 pad.5.mult_ref
  18.8 0.0 copy-start.2
  18.8 148.7 %fine.1 = f32[165,2048]{1,0:T(8,128)} custom-call(f32[176,2048]{1,0:T(8,128)} %pad.5.mult_ref, f32[32,165,165]{2,1,0:T(8,128)} %copy.9.ops_ref, s32[8,16]{1,0:T(8,128)} %bitcast.15, s32[32,32]{1,0:T(8,128)} %lists_ref.1, s32[1]{0:T(128)S(6)} %copy.14.live_ref), custom_call_target="tpu_custom_call" | custom-call | flops 14273740800 | bytes 8388608 | tf_op jit(solution)/shard_map/fine/pallas_call | solution.py:239
  167.6 0.0 copy-done.2
  167.6 0.0 all-gather.2.cloned.1.call-done
  167.6 11.4 %concatenate.3 = f32[16385,165]{1,0:T(8,128)} pad(f32[16384,165]{1,0:T(8,128)} %all-gather.2.cloned.1.call-done, f32[]{:T(128)} %constant.7.clone.1), padding=0_1x0_0 | pad | bytes 21627544 | tf_op jit(solution)/shard_map/concatenate | solution.py:17
  179.0 12.4 %gather_fusion = f32[2048,165]{1,0:T(8,128)S(1)} fusion(f32[16385,165]{1,0:T(8,128)} %concatenate.3, s32[2048]{0:T(1024)S(1)} %broadcast_clamp_fusion), kind=kCustom, calls=%fused_computation | custom fusion | bytes 2711552 | tf_op jit(solution)/shard_map/jit(_take)/gather | solution.py:19
  191.4 0.0 copy-start.1
  191.4 9.0 %fusion.2 = f32[165,64]{0,1:T(8,128)} fusion(f32[32,64,165]{2,1,0:T(8,128)S(1)} %bitcast.12, pred[32,64]{1,0:T(8,128)(4,1)S(1)} %compare_and_fusion, f32[32,165,165]{2,0,1:T(8,128)} %param.9), kind=kOutput, calls=%fused_computation.3 | convolution fusion | flops 334878720 | bytes 4880768 | tf_op jit(solution)/shard_map/jcd,jtd->ct/dot_general | solution.py:22
  200.5 0.0 copy-done.1
  200.5 1.1 copy.15
  (3 shorter events, 0.0 us)
Async XLA Ops:
  7.2 160.5 %all-gather.2.cloned.1.call-start = ((), (), s32[]{:S(2)}) async-start(), calls=%async_computation | async-start | bytes 16842752 | tf_op jit(solution)/shard_map/all_gather | solution.py:265
  8.7 8.8 %copy-start = (f32[165,2048]{1,0:T(8,128)S(1)}, f32[165,2048]{1,0:T(8,128)}, u32[]{:S(2)}) copy-start(f32[165,2048]{1,0:T(8,128)} %param.7) | copy-start | bytes 4055044
  18.8 148.8 %copy-start.2 = (s32[64,32]{0,1:T(8,128)S(1)}, s32[64,32]{0,1:T(8,128)}, u32[]{:S(2)}) copy-start(s32[64,32]{0,1:T(8,128)} %param.11) | copy-start | bytes 24580
  191.4 9.1 %copy-start.1 = (f32[165,2048]{1,0:T(8,128)S(1)}, f32[165,2048]{1,0:T(8,128)}, u32[]{:S(2)}) copy-start(f32[165,2048]{1,0:T(8,128)} %fine.1) | copy-start | bytes 4055044
Sparse Core Ops, SparseCore 0:
  11.6 143.4 all-gather.1

commit v2 on v1

--- a/solution.py
+++ b/solution.py
@@ -8,24 +8,16 @@
 
 BCELLS = 64
 ROWS = 16
+XCHIPS = 4
+WIDTH = 42
+PARTS = 3
+PACKED = 24
+CHUNK = 4
+Y_TICK = 3
+CORE_TICK = 8
+ARRANGE_TICK = 4
+COARSE_TICK = 11
 MESH = pl.DeviceIdType.MESH
-
-
-def coarse_terms(operators, everything, coarse_lists):
-    coef_rows = everything.shape[1]
-    count = everything.shape[0]
-    extended = jnp.concatenate([everything, jnp.zeros((1, coef_rows), everything.dtype)], axis=0)
-    safe = jnp.where(coarse_lists < 0, count, coarse_lists)
-    taken = jnp.take(extended, safe.T.reshape(-1), axis=0).reshape(
-        operators.shape[0], -1, coef_rows
-    )
-    return jnp.einsum(
-        "jcd,jtd->ct",
-        operators,
-        taken,
-        precision=lax.Precision.HIGH,
-        preferred_element_type=jnp.float32,
-    )
 
 
 def lanes_below(shape, limit):
@@ -34,13 +26,83 @@
 
 def fine_kernel(
     groups, steps, own, sent, low_bits, offsets,
-    mult_ref, ops_ref, send_ref, lists_ref, live_ref,
-    out_ref,
-    table, outgo, landed, split, mats, total, send_sem, recv_sem,
+    mult_ref, coarse_ref, ops_hbm, codes_ref, send_ref, lists_ref, live_ref,
+    out_ref, coarse_out_ref,
+    table, outgo, landed, split, mats, total, ops_ref,
+    packed, everything, codes, codes_smem, replicas, gathered, partial, incoming,
+    send_sem, recv_sem, ops_sem, slice_send, slice_recv, code_send, code_recv,
+    z_send, z_recv, y_send, y_recv, core_send, core_recv, sum_send, sum_recv, smem_sem,
 ):
     slots, coef, _ = ops_ref.shape
     gx = lax.axis_index("gx")
     gy = lax.axis_index("gy")
+    chip, core = gx // 2, lax.rem(gx, 2)
+    z, y = gy // 4, lax.rem(gy, 4)
+    cells = coarse_ref.shape[0]
+
+    def x_peer(o):
+        return lax.rem(chip + o, XCHIPS)
+
+    def x_device(o):
+        return (x_peer(o) * 2 + core, gy)
+
+    def z_device(o):
+        return (gx, lax.rem(z + o, 8) * 4 + y)
+
+    def y_device(o):
+        return (gx, z * 4 + lax.rem(y + o, 4))
+
+    def core_device():
+        return (gx + 1 - 2 * core, gy)
+
+    def rows_of(c, yy, zz, xx, count):
+        at = (((c * 4 + yy) * 8 + zz) * XCHIPS + xx) * PACKED
+        return pl.ds(pl.multiple_of(at, 8), count * PACKED)
+
+    def remote(source, target, send, recv, device):
+        return pltpu.make_async_remote_copy(
+            src_ref=source, dst_ref=target, send_sem=send, recv_sem=recv,
+            device_id=device, device_id_type=MESH,
+        )
+
+    def slice_copy(o):
+        return remote(
+            packed.at[x_peer(o)], everything.at[rows_of(core, y, z, chip, 1)],
+            slice_send.at[o - 1], slice_recv.at[o - 1], x_device(o),
+        )
+
+    def code_copy(o):
+        return remote(
+            codes_ref, codes.at[chip], code_send.at[o - 1], code_recv.at[o - 1], x_device(o)
+        )
+
+    def z_copy(o):
+        rows = rows_of(core, y, z, 0, XCHIPS)
+        return remote(
+            everything.at[rows], everything.at[rows], z_send.at[o - 1], z_recv.at[o - 1], z_device(o)
+        )
+
+    def y_copy(o):
+        rows = rows_of(core, y, 0, 0, 8 * XCHIPS)
+        return remote(
+            everything.at[rows], everything.at[rows], y_send.at[o - 1], y_recv.at[o - 1], y_device(o)
+        )
+
+    def core_copy():
+        rows = rows_of(core, 0, 0, 0, 32 * XCHIPS)
+        return remote(everything.at[rows], everything.at[rows], core_send, core_recv, core_device())
+
+    def sum_copy(o):
+        return remote(
+            partial.at[x_peer(o)], incoming.at[chip],
+            sum_send.at[o - 1], sum_recv.at[o - 1], x_device(o),
+        )
+
+    def ops_copy(j):
+        return pltpu.make_async_copy(ops_hbm.at[:, j, :], ops_ref.at[j], ops_sem.at[j])
+
+    def codes_copy():
+        return pltpu.make_async_copy(codes.at[:, 0:slots], codes_smem, smem_sem)
 
     def partner(k):
         if k < low_bits:
@@ -62,25 +124,67 @@
         )
 
     barrier = pltpu.get_barrier_semaphore()
-    for k in range(steps):
-        pl.semaphore_signal(barrier, inc=1, device_id=partner(k), device_id_type=MESH)
+    peers = [x_device(o) for o in range(1, XCHIPS)] + [z_device(o) for o in range(1, 8)]
+    peers += [y_device(o) for o in range(1, 4)] + [core_device()]
+    for peer in peers:
+        pl.semaphore_signal(barrier, inc=1, device_id=peer, device_id_type=MESH)
+    lax.fori_loop(0, slots, lambda j, c: (ops_copy(j).start(), c)[1], 0)
+
+    lane64 = lax.broadcasted_iota(jnp.int32, (cells, 128), 1)
+    near = coarse_ref[:, :128]
+    far = jnp.concatenate(
+        [coarse_ref[:, 128:], jnp.zeros((cells, 256 - coef), jnp.float32)], axis=1
+    )
+    for x in range(XCHIPS):
+        shift = (128 - WIDTH * x) % 128
+        base = pltpu.roll(near, shift, 1) if shift else near
+        if x == XCHIPS - 1:
+            base = jnp.where(lane64 < shift, base, pltpu.roll(far, shift, 1))
+        base = jnp.where(lane64 < WIDTH, base, 0.0)
+        rest = jnp.concatenate(
+            [base[2 * PACKED :], jnp.zeros((3 * PACKED - cells, 128), jnp.float32)], axis=0
+        )
+        packed[x] = (
+            base[:PACKED]
+            + pltpu.roll(base[PACKED : 2 * PACKED], WIDTH, 1)
+            + pltpu.roll(rest, 2 * WIDTH, 1)
+        )
+    everything[rows_of(core, y, z, chip, 1)] = packed[chip]
+    codes[chip] = codes_ref[...]
 
     half = lanes_below((8, 128), 64)
 
-    def own_blocks(g, carry):
+    def place(g, p, first, second):
+        table[g, 2 * p] = jnp.where(half, first, pltpu.roll(second, 64, 1))
+        table[g, 2 * p + 1] = jnp.where(half, pltpu.roll(first, 64, 1), second)
+
+    def own_blocks(g):
         def pair(p, c):
             lanes = pl.ds(pl.multiple_of(p * 128, 128), 128)
             first = mult_ref[pl.ds(pl.multiple_of(g * ROWS, 8), 8), lanes]
             second = mult_ref[pl.ds(pl.multiple_of(g * ROWS + 8, 8), 8), lanes]
-            table[g, 2 * p] = jnp.where(half, first, pltpu.roll(second, 64, 1))
-            table[g, 2 * p + 1] = jnp.where(half, pltpu.roll(first, 64, 1), second)
+            place(g, p, first, second)
             return c
 
-        return lax.fori_loop(0, own // 2, pair, carry, unroll=True)
-
-    lax.fori_loop(0, groups, own_blocks, 0)
+        lax.fori_loop(0, own // 2, pair, 0, unroll=True)
+
+    def last_blocks():
+        g = groups - 1
+        left = coef - g * ROWS
+
+        def pair(p, c):
+            lanes = pl.ds(pl.multiple_of(p * 128, 128), 128)
+            first = jnp.concatenate(
+                [mult_ref[g * ROWS : coef, lanes], jnp.zeros((8 - left, 128), jnp.float32)], axis=0
+            )
+            place(g, p, first, jnp.zeros((8, 128), jnp.float32))
+            return c
+
+        lax.fori_loop(0, own // 2, pair, 0)
+
+    own_blocks(0)
     split[0] = jnp.zeros((ROWS, 128), jnp.bfloat16)
-    pl.semaphore_wait(barrier, steps)
+    pl.semaphore_wait(barrier, len(peers))
 
     def send(g, k):
         if k > 0:
@@ -95,6 +199,9 @@
         per = 128 // ROWS
         lane = lax.broadcasted_iota(jnp.int32, (ROWS, 128), 1)
         tail = coef - 128
+        beyond = (lane >= 2) & (jnp.full((ROWS, 128), chip, jnp.int32) == XCHIPS - 1)
+        for i in range(per):
+            ops_copy(q * per + i).wait()
 
         def rows_at(read, at):
             tiles = []
@@ -108,6 +215,17 @@
                         ),
                     )
                 )
+            height = mats.shape[1] // 2
+            for i in range(per):
+                base = pltpu.roll(tiles[i][0], lax.rem(128 - WIDTH * chip, 128), 1)
+                base = jnp.where(beyond, pltpu.roll(tiles[i][1], 2, 1), base)
+                base = jnp.where(lane < WIDTH, base, 0.0)
+                base = base + pltpu.roll(base, WIDTH, 1) + pltpu.roll(base, 2 * WIDTH, 1)
+                high = base.astype(jnp.bfloat16)
+                low = (base - high.astype(jnp.float32)).astype(jnp.bfloat16)
+                lanes = pl.ds(pl.multiple_of((q * per + i) * 128, 128), 128)
+                replicas[pl.ds(at, ROWS), lanes] = high
+                replicas[pl.ds(height + at, ROWS), lanes] = low
             for g in range(groups):
                 which, at_lane = divmod(g * ROWS, 128)
                 value = jnp.zeros((ROWS, 128), jnp.float32)
@@ -119,7 +237,6 @@
                     value = jnp.where((lane >= i * ROWS) & (lane < (i + 1) * ROWS), piece, value)
                 high = value.astype(jnp.bfloat16)
                 low = (value - high.astype(jnp.float32)).astype(jnp.bfloat16)
-                height = mats.shape[1] // 2
                 mats[g, pl.ds(at, ROWS), pl.ds(pl.multiple_of(q * 128, 128), 128)] = high
                 mats[g, pl.ds(height + at, ROWS), pl.ds(pl.multiple_of(q * 128, 128), 128)] = low
 
@@ -178,9 +295,78 @@
 
         lax.fori_loop(0, own // 2, targets, 0)
 
+    lane = lax.broadcasted_iota(jnp.int32, (cells, 128), 1)
+    part_of = jnp.where(lane < WIDTH, 0, jnp.where(lane < 2 * WIDTH, 1, jnp.where(lane < 3 * WIDTH, 2, 7)))
+
+    def coarse_chunk(c):
+        for i in range(CHUNK):
+            def take(n, carry):
+                x, first = n // (cells // 16), lax.rem(n, cells // 16) * 16
+                for r in range(16):
+                    code = codes_smem[x, c * CHUNK + i, first + r]
+                    gathered[i, pl.ds(n * 16 + r, 1), :] = everything[
+                        pl.ds(lax.shift_right_logical(code, 2), 1), :
+                    ]
+                return carry
+
+            lax.fori_loop(0, XCHIPS * cells // 16, take, 0)
+        highs, lows = [], []
+        for x in range(XCHIPS):
+            turned = pltpu.roll(codes[x, slots : slots + cells, :], lax.rem(128 - c * CHUNK, 128), 1)
+            row_high, row_low = [], []
+            for i in range(CHUNK):
+                value = gathered[i, x * cells : (x + 1) * cells]
+                value = jnp.where(part_of == (turned[:, i : i + 1] & 3), value, 0.0)
+                high = value.astype(jnp.bfloat16)
+                row_high.append(high)
+                row_low.append((value - high.astype(jnp.float32)).astype(jnp.bfloat16))
+            highs.append(jnp.concatenate(row_high, axis=1))
+            lows.append(jnp.concatenate(row_low, axis=1))
+        high = jnp.concatenate(highs, axis=0)
+        low = jnp.concatenate(lows, axis=0)
+        height = mats.shape[1] // 2
+        lanes = pl.ds(pl.multiple_of(c * CHUNK * 128, CHUNK * 128), CHUNK * 128)
+        op_high = replicas[:height, lanes]
+        op_low = replicas[height:, lanes]
+        dims = (((1,), (1,)), ((), ()))
+
+        def dot(a, b):
+            return lax.dot_general(a, b, dims, preferred_element_type=jnp.float32)
+
+        product = dot(high, op_high) + dot(low, op_high) + dot(high, op_low)
+        for x in range(XCHIPS):
+            partial[x] += product[x * cells : (x + 1) * cells]
+
+    for o in range(1, XCHIPS):
+        slice_copy(o).start()
+        code_copy(o).start()
     total[...] = jnp.zeros_like(total)
+    partial[...] = jnp.zeros_like(partial)
 
     def tick(s, carry):
+        @pl.when(s == 1)
+        def _():
+            for o in range(1, XCHIPS):
+                slice_copy(o).wait_recv()
+            for o in range(1, 8):
+                z_copy(o).start()
+
+        @pl.when(s == Y_TICK)
+        def _():
+            for o in range(1, 8):
+                z_copy(o).wait_recv()
+            for o in range(1, 4):
+                y_copy(o).start()
+
+        @pl.when(s == CORE_TICK)
+        def _():
+            for o in range(1, 4):
+                y_copy(o).wait_recv()
+            core_copy().start()
+            for o in range(1, XCHIPS):
+                code_copy(o).wait_recv()
+            codes_copy().start()
+
         for k in reversed(range(steps)):
             g = s - offsets[k]
 
@@ -188,9 +374,31 @@
             def _():
                 send(g, k)
 
-        @pl.when(s < slots * ROWS // 128)
-        def _():
-            arrange(s)
+        @pl.when(s < groups - 2)
+        def _():
+            own_blocks(s + 1)
+
+        @pl.when(s == groups - 2)
+        def _():
+            last_blocks()
+
+        @pl.when((s >= ARRANGE_TICK) & (s < ARRANGE_TICK + slots * ROWS // 128))
+        def _():
+            arrange(s - ARRANGE_TICK)
+
+        @pl.when(s == COARSE_TICK)
+        def _():
+            core_copy().wait_recv()
+            codes_copy().wait()
+
+        @pl.when((s >= COARSE_TICK) & (s < COARSE_TICK + slots // CHUNK))
+        def _():
+            coarse_chunk(s - COARSE_TICK)
+
+        @pl.when(s == COARSE_TICK + slots // CHUNK - 1)
+        def _():
+            for o in range(1, XCHIPS):
+                sum_copy(o).start()
 
         g = s - offsets[steps]
 
@@ -208,6 +416,20 @@
         return carry
 
     lax.fori_loop(0, groups, drain, 0)
+
+    for o in range(1, XCHIPS):
+        sum_copy(o).wait_recv()
+    coarse_out_ref[...] = (
+        (partial[chip] + incoming[x_peer(1)]) + (incoming[x_peer(2)] + incoming[x_peer(3)])
+    )[:, :coef]
+    for o in range(1, XCHIPS):
+        slice_copy(o).wait_send()
+        code_copy(o).wait_send()
+        sum_copy(o).wait_send()
+        y_copy(o).wait_send()
+    for o in range(1, 8):
+        z_copy(o).wait_send()
+    core_copy().wait_send()
 
     live = live_ref[0]
     side = lanes_below((coef, 128), 64)
@@ -225,47 +447,91 @@
     lax.fori_loop(0, own // 2, finish, 0)
 
 
-def fine_part(multipoles, operators, block_lists, send_lists, live_blocks):
+def source_codes(coarse_lists):
+    cells, slots = coarse_lists.shape
+    index = jnp.maximum(coarse_lists, 0)
+    cell, device = index % cells, index // cells
+    gy, gx = device % 32, device // 32
+    place = (((gx % 2) * 4 + gy % 4) * 8 + gy // 4) * XCHIPS + gx // 2
+    code = (place * PACKED + cell % PACKED) * 4 + cell // PACKED
+    code = jnp.where(coarse_lists < 0, 3, code).astype(jnp.int32)
+    by_slot = jnp.pad(code.T, ((0, 0), (0, 128 - cells)))
+    by_cell = jnp.pad(code, ((0, 0), (0, 128 - slots)))
+    return jnp.concatenate([by_slot, by_cell], axis=0)
+
+
+def shards(multipoles, coarse_poles, operators, block_lists, coarse_lists, send_lists, live_blocks):
     coef, cells = multipoles.shape
     slots = operators.shape[0]
+    coarse_cells = coarse_poles.shape[1]
     own = cells // BCELLS
     _, steps, sent = send_lists.shape
     groups = -(-coef // ROWS)
+    height = groups * ROWS
+    held = own + steps * sent
     low_bits = lax.axis_size("gy").bit_length() - 1
-    offsets = tuple(range(steps + 1))
-    padded = jnp.pad(multipoles, ((0, groups * ROWS - coef), (0, 0)))
+    offsets = (0, 1, 2, 4, 6, 8, 9, 10, 11)
     vmem = pl.BlockSpec(memory_space=pltpu.VMEM)
     smem = pl.BlockSpec(memory_space=pltpu.SMEM)
-    return pl.pallas_call(
+    f32, bf16, dma = jnp.float32, jnp.bfloat16, pltpu.SemaphoreType.DMA
+    fine_local, coarse_local = pl.pallas_call(
         functools.partial(fine_kernel, groups, steps, own, sent, low_bits, offsets),
-        out_shape=jax.ShapeDtypeStruct((coef, cells), jnp.float32),
-        in_specs=[vmem, vmem, smem, smem, smem],
-        out_specs=vmem,
+        out_shape=(
+            jax.ShapeDtypeStruct((coef, cells), f32),
+            jax.ShapeDtypeStruct((coarse_cells, coef), f32),
+        ),
+        in_specs=[vmem, vmem, pl.BlockSpec(memory_space=pl.ANY), vmem, smem, smem, smem],
+        out_specs=(vmem, vmem),
         scratch_shapes=[
-            pltpu.VMEM((groups, own + steps * sent, 8, 128), jnp.float32),
-            pltpu.VMEM((groups, steps, sent, 8, 128), jnp.float32),
-            pltpu.VMEM((groups, steps, sent, 8, 128), jnp.float32),
-            pltpu.VMEM((own + steps * sent + 1, ROWS, 128), jnp.bfloat16),
-            pltpu.VMEM((groups, 2 * groups * ROWS, slots * ROWS), jnp.bfloat16),
-            pltpu.VMEM((groups * ROWS, own * 128), jnp.float32),
-            pltpu.SemaphoreType.DMA((groups, steps)),
-            pltpu.SemaphoreType.DMA((groups, steps)),
+            pltpu.VMEM((groups, held, 8, 128), f32),
+            pltpu.VMEM((groups, steps, sent, 8, 128), f32),
+            pltpu.VMEM((groups, steps, sent, 8, 128), f32),
+            pltpu.VMEM((held + 1, ROWS, 128), bf16),
+            pltpu.VMEM((groups, 2 * height, slots * ROWS), bf16),
+            pltpu.VMEM((height, own * 128), f32),
+            pltpu.VMEM((slots, coef, coef), f32),
+            pltpu.VMEM((XCHIPS, PACKED, 128), f32),
+            pltpu.VMEM((64 * XCHIPS * PACKED, 128), f32),
+            pltpu.VMEM((XCHIPS, slots + coarse_cells, 128), jnp.int32),
+            pltpu.SMEM((XCHIPS, slots, 128), jnp.int32),
+            pltpu.VMEM((2 * height, slots * 128), bf16),
+            pltpu.VMEM((CHUNK, XCHIPS * coarse_cells, 128), f32),
+            pltpu.VMEM((XCHIPS, coarse_cells, height), f32),
+            pltpu.VMEM((XCHIPS, coarse_cells, height), f32),
+            dma((groups, steps)),
+            dma((groups, steps)),
+            dma((slots,)),
+            dma((XCHIPS - 1,)),
+            dma((XCHIPS - 1,)),
+            dma((XCHIPS - 1,)),
+            dma((XCHIPS - 1,)),
+            dma((7,)),
+            dma((7,)),
+            dma((3,)),
+            dma((3,)),
+            dma,
+            dma,
+            dma((XCHIPS - 1,)),
+            dma((XCHIPS - 1,)),
+            dma,
         ],
         compiler_params=pltpu.CompilerParams(
-            collective_id=0, has_side_effects=True, vmem_limit_bytes=60 << 20
+            collective_id=0, has_side_effects=True, vmem_limit_bytes=62 << 20
         ),
         cost_estimate=pl.CostEstimate(
             flops=8 * slots * coef * coef * cells, bytes_accessed=8 << 20, transcendentals=0
         ),
-        name="fine",
-    )(padded, operators, send_lists[0], block_lists, live_blocks)
-
-
-def shards(multipoles, coarse_poles, operators, block_lists, coarse_lists, send_lists, live_blocks):
-    everything = lax.all_gather(coarse_poles.T, ("gx", "gy"), axis=0, tiled=True)
-    fine_local = fine_part(multipoles, operators, block_lists, send_lists, live_blocks)
-    coarse_local = coarse_terms(operators, everything, coarse_lists)
-    return (fine_local, coarse_local)
+        name="far_field",
+    )(
+        multipoles,
+        coarse_poles.T,
+        operators.transpose(1, 0, 2),
+        source_codes(coarse_lists),
+        send_lists[0],
+        block_lists,
+        live_blocks,
+    )
+    return (fine_local, coarse_local.T)
 
 
 def solution(mesh):

time: 211 us -> 188 us (0.89)
  Pallas kernels: 149 us -> 180 us
  local copies, waits for them, and re-layouts: 34.4 us -> 4.08 us
  between operations: 14.8 us -> 1.3 us
  matrix products: 9.05 us -> 0 us
    pallas_call x1, Pallas kernels: 149 us -> 180 us  [shards(): pl.pallas_call(functools.partial(fine_kernel, groups, steps, own, sent, l...]
    gather x1 -> x0, local copies, waits for them, and re-layouts: 12.4 us -> none  [coarse_terms(): jnp.take(extended, safe.T.reshape(-1), axis=0)]
    concatenate x1 -> x0, local copies, waits for them, and re-layouts: 11.4 us -> none  [coarse_terms(): jnp.concatenate([everything, jnp.zeros((1, coef_rows), everything.dtype)]...]
    dot_general x1 -> x0, matrix products: 9.05 us -> none  [coarse_terms(): jnp.einsum('jcd,jtd->ct', operators, taken, precision=lax.Precision.HIGH,...]
    unnamed x8 -> x6, local copies, waits for them, and re-layouts: 9.26 us -> 4.08 us
  transfers between devices with their start and end apart: 1 -> 0, of which waited for: 0 -> 0; matrix products, arithmetic and copies ran while one was open for 5% -> 0% of each run, Pallas kernels for 71% -> 0%
where the time goes in v2:
time: 188 us; the launch traced here: 186 us
  Pallas kernels  180 us (96%)
  local copies, waits for them, and re-layouts  4.08 us (2%)
    pallas_call x1, Pallas kernels, shards(): pl.pallas_call(functools.partial(fine_kernel, groups, steps, own, sent, l...  180 us
    unnamed x6, local copies, waits for them, and re-layouts  4.08 us

profile of v2, /device:TPU:8, one launch (start us, length us, event | category | flops | bytes accessed | tf_op | source)
XLA Modules:
  0.0 185.9 jit_solution(7058909496565000283)
XLA Ops:
  1.3 0.8 copy.9
  2.1 0.2 fusion.23
  2.2 0.1 copy.12
  2.3 0.2 fusion.10
  2.5 0.6 pad_add_fusion.codes_ref
  3.1 179.6 %far_field.1 = (f32[165,2048]{1,0:T(8,128)}, f32[64,165]{1,0:T(8,128)}) custom-call(f32[165,2048]{1,0:T(8,128)} %mult_ref.1, f32[64,165]{1,0:T(8,128)} %bitcast.8, f32[165,32,165]{2,1,0:T(8,128)} %bitcast.7, s32[96,128]{1,0:T(8,128)} %pad_add_fusion.codes_ref, s32[8,16]{1,0:T(8,128)} %bitcast.9, s32[32,32]{1,0:T(8,128)} %lists_ref.1, s32[1]{0:T(128)S(6)} %copy.15.live_ref), custom_call_target="tpu_custom_call" | custom-call | flops 14273740800 | bytes 8388608 | tf_op jit(solution)/shard_map/far_field/pallas_call | solution.py:477
  182.7 0.0 copy-start
  182.7 2.6 %copy.16 = f32[165,2048]{1,0:T(8,128)} copy(f32[165,2048]{1,0:T(8,128)} %get-tuple-element.8) | data formatting | bytes 2703360
  185.3 0.0 copy-done
  185.3 0.6 copy.17
Async XLA Ops:
  182.7 2.6 %copy-start = (f32[64,165]{1,0:T(8,128)S(1)}, f32[64,165]{1,0:T(8,128)}, u32[]{:S(2)}) copy-start(f32[64,165]{1,0:T(8,128)} %get-tuple-element.5) | copy-start | bytes 126724

commit v3 on v2

--- a/solution.py
+++ b/solution.py
@@ -13,10 +13,11 @@
 PARTS = 3
 PACKED = 24
 CHUNK = 4
-Y_TICK = 3
-CORE_TICK = 8
-ARRANGE_TICK = 4
-COARSE_TICK = 11
+WIDE = 16
+STRIDE = 2
+OFFSETS = (0, 2, 4, 6, 9, 13, 15, 17, 19)
+X_TICK, Y_TICK, CORE_TICK, COARSE_TICK = 2, 5, 12, 20
+ARRANGE_TICK, ARRANGE_STEP = 4, 4
 MESH = pl.DeviceIdType.MESH
 
 
@@ -195,13 +196,12 @@
             outgo[g, k, i] = table[g, send_ref[k, i]]
         copy(g, k).start()
 
-    def arrange(q):
+    def arrange(n):
+        q, at = n // groups, pl.multiple_of(lax.rem(n, groups) * ROWS, ROWS)
         per = 128 // ROWS
         lane = lax.broadcasted_iota(jnp.int32, (ROWS, 128), 1)
         tail = coef - 128
         beyond = (lane >= 2) & (jnp.full((ROWS, 128), chip, jnp.int32) == XCHIPS - 1)
-        for i in range(per):
-            ops_copy(q * per + i).wait()
 
         def rows_at(read, at):
             tiles = []
@@ -241,24 +241,24 @@
                 mats[g, pl.ds(height + at, ROWS), pl.ds(pl.multiple_of(q * 128, 128), 128)] = low
 
         whole = coef // ROWS
-
-        def body(r, c):
-            at = pl.multiple_of(r * ROWS, ROWS)
+        left = coef - whole * ROWS
+
+        @pl.when(lax.rem(n, groups) < whole)
+        def _():
             rows_at(lambda j: ops_ref[j, pl.ds(at, ROWS), :], at)
-            return c
-
-        lax.fori_loop(0, whole, body, 0)
-        left = coef - whole * ROWS
-        rows_at(
-            lambda j: jnp.concatenate(
-                [
-                    ops_ref[j, whole * ROWS : coef, :],
-                    jnp.zeros((ROWS - left, coef), jnp.float32),
-                ],
-                axis=0,
-            ),
-            whole * ROWS,
-        )
+
+        @pl.when(lax.rem(n, groups) == whole)
+        def _():
+            rows_at(
+                lambda j: jnp.concatenate(
+                    [
+                        ops_ref[j, whole * ROWS : coef, :],
+                        jnp.zeros((ROWS - left, coef), jnp.float32),
+                    ],
+                    axis=0,
+                ),
+                whole * ROWS,
+            )
 
     def multiply(g):
         copy(g, steps - 1).wait_recv()
@@ -276,47 +276,46 @@
             split[pl.ds(at + 1, 16)] = jnp.concatenate([top, bottom], axis=1).astype(jnp.bfloat16)
             return carry
 
-        lax.fori_loop(0, (own + steps * sent) // 16, cut, 0)
+        lax.fori_loop(0, (own + steps * sent) // 16, cut, 0, unroll=True)
         height = mats.shape[1] // 2
 
         def targets(p, carry):
             sides = []
-            for side in range(2):
+            for side in range(WIDE):
                 sides.append(
                     jnp.concatenate(
-                        [split[lists_ref[2 * p + side, j] + 1] for j in range(slots)], axis=0
+                        [split[lists_ref[WIDE * p + side, j] + 1] for j in range(slots)], axis=0
                     )
                 )
             source = jnp.concatenate(sides, axis=1)
             product = jnp.dot(mats[g], source, preferred_element_type=jnp.float32)
-            lanes = pl.ds(pl.multiple_of(p * 256, 256), 256)
+            lanes = pl.ds(pl.multiple_of(p * WIDE * 128, WIDE * 128), WIDE * 128)
             total[:, lanes] += product[:height] + product[height:]
             return carry
 
-        lax.fori_loop(0, own // 2, targets, 0)
+        lax.fori_loop(0, own // WIDE, targets, 0)
 
     lane = lax.broadcasted_iota(jnp.int32, (cells, 128), 1)
     part_of = jnp.where(lane < WIDTH, 0, jnp.where(lane < 2 * WIDTH, 1, jnp.where(lane < 3 * WIDTH, 2, 7)))
 
     def coarse_chunk(c):
         for i in range(CHUNK):
-            def take(n, carry):
-                x, first = n // (cells // 16), lax.rem(n, cells // 16) * 16
-                for r in range(16):
-                    code = codes_smem[x, c * CHUNK + i, first + r]
-                    gathered[i, pl.ds(n * 16 + r, 1), :] = everything[
-                        pl.ds(lax.shift_right_logical(code, 2), 1), :
+            def take(x, carry, i=i):
+                for r in range(cells):
+                    row = codes_smem[x, c * CHUNK + i, r]
+                    gathered[i, pl.ds(pl.multiple_of(x * cells, 8) + r, 1), :] = everything[
+                        pl.ds(row, 1), :
                     ]
                 return carry
 
-            lax.fori_loop(0, XCHIPS * cells // 16, take, 0)
+            lax.fori_loop(0, XCHIPS, take, 0)
         highs, lows = [], []
         for x in range(XCHIPS):
             turned = pltpu.roll(codes[x, slots : slots + cells, :], lax.rem(128 - c * CHUNK, 128), 1)
             row_high, row_low = [], []
             for i in range(CHUNK):
                 value = gathered[i, x * cells : (x + 1) * cells]
-                value = jnp.where(part_of == (turned[:, i : i + 1] & 3), value, 0.0)
+                value = jnp.where(part_of == turned[:, i : i + 1], value, 0.0)
                 high = value.astype(jnp.bfloat16)
                 row_high.append(high)
                 row_low.append((value - high.astype(jnp.float32)).astype(jnp.bfloat16))
@@ -344,7 +343,7 @@
     partial[...] = jnp.zeros_like(partial)
 
     def tick(s, carry):
-        @pl.when(s == 1)
+        @pl.when(s == X_TICK)
         def _():
             for o in range(1, XCHIPS):
                 slice_copy(o).wait_recv()
@@ -368,23 +367,33 @@
             codes_copy().start()
 
         for k in reversed(range(steps)):
-            g = s - offsets[k]
-
-            @pl.when((g >= 0) & (g < groups))
+            late = s - offsets[k]
+            g = late // STRIDE
+
+            @pl.when((late >= 0) & (g < groups) & (lax.rem(late, STRIDE) == 0))
             def _():
                 send(g, k)
 
-        @pl.when(s < groups - 2)
-        def _():
-            own_blocks(s + 1)
-
-        @pl.when(s == groups - 2)
+        g = s // STRIDE + 1
+
+        @pl.when((g < groups - 1) & (lax.rem(s, STRIDE) == 0))
+        def _():
+            own_blocks(g)
+
+        @pl.when((g == groups - 1) & (lax.rem(s, STRIDE) == 0))
         def _():
             last_blocks()
 
-        @pl.when((s >= ARRANGE_TICK) & (s < ARRANGE_TICK + slots * ROWS // 128))
-        def _():
-            arrange(s - ARRANGE_TICK)
+        @pl.when(s == ARRANGE_TICK)
+        def _():
+            lax.fori_loop(0, slots, lambda j, c: (ops_copy(j).wait(), c)[1], 0)
+
+        first = (s - ARRANGE_TICK) * ARRANGE_STEP
+        last = jnp.minimum(first + ARRANGE_STEP, groups * slots * ROWS // 128)
+
+        @pl.when(first >= 0)
+        def _():
+            lax.fori_loop(first, last, lambda n, c: (arrange(n), c)[1], 0)
 
         @pl.when(s == COARSE_TICK)
         def _():
@@ -400,15 +409,16 @@
             for o in range(1, XCHIPS):
                 sum_copy(o).start()
 
-        g = s - offsets[steps]
-
-        @pl.when((g >= 0) & (g < groups))
+        late = s - offsets[steps]
+        g = late // STRIDE
+
+        @pl.when((late >= 0) & (g < groups) & (lax.rem(late, STRIDE) == 0))
         def _():
             multiply(g)
 
         return carry
 
-    lax.fori_loop(0, groups + offsets[steps], tick, 0)
+    lax.fori_loop(0, (groups - 1) * STRIDE + offsets[steps] + 1, tick, 0)
 
     def drain(g, carry):
         for k in range(steps):
@@ -453,10 +463,10 @@
     cell, device = index % cells, index // cells
     gy, gx = device % 32, device // 32
     place = (((gx % 2) * 4 + gy % 4) * 8 + gy // 4) * XCHIPS + gx // 2
-    code = (place * PACKED + cell % PACKED) * 4 + cell // PACKED
-    code = jnp.where(coarse_lists < 0, 3, code).astype(jnp.int32)
-    by_slot = jnp.pad(code.T, ((0, 0), (0, 128 - cells)))
-    by_cell = jnp.pad(code, ((0, 0), (0, 128 - slots)))
+    row = (place * PACKED + cell % PACKED).astype(jnp.int32)
+    part = jnp.where(coarse_lists < 0, PARTS, cell // PACKED).astype(jnp.int32)
+    by_slot = jnp.pad(row.T, ((0, 0), (0, 128 - cells)))
+    by_cell = jnp.pad(part, ((0, 0), (0, 128 - slots)))
     return jnp.concatenate([by_slot, by_cell], axis=0)
 
 
@@ -470,7 +480,7 @@
     height = groups * ROWS
     held = own + steps * sent
     low_bits = lax.axis_size("gy").bit_length() - 1
-    offsets = (0, 1, 2, 4, 6, 8, 9, 10, 11)
+    offsets = OFFSETS
     vmem = pl.BlockSpec(memory_space=pltpu.VMEM)
     smem = pl.BlockSpec(memory_space=pltpu.SMEM)
     f32, bf16, dma = jnp.float32, jnp.bfloat16, pltpu.SemaphoreType.DMA

time: 188 us -> 143 us (0.76); the launches traced: 186 us -> 143 us
  Pallas kernels: 180 us -> 137 us
    pallas_call x1, Pallas kernels: 180 us -> 137 us  [shards(): pl.pallas_call(functools.partial(fine_kernel, groups, steps, own, sent, l...]
where the time goes in v3:
time: 143 us
  Pallas kernels  137 us (96%)
  local copies, waits for them, and re-layouts  4.08 us (3%)
    pallas_call x1, Pallas kernels, shards(): pl.pallas_call(functools.partial(fine_kernel, groups, steps, own, sent, l...  137 us
    unnamed x6, local copies, waits for them, and re-layouts  4.08 us

profile of v3, /device:TPU:8, one launch (start us, length us, event | category | flops | bytes accessed | tf_op | source)
XLA Modules:
  0.0 143.2 jit_solution(15049259452715000549)
XLA Ops:
  1.3 0.8 copy.9
  2.1 0.2 fusion.8
  2.2 0.1 copy.12
  2.3 0.6 pad_add_fusion.codes_ref
  2.9 137.0 %far_field.1 = (f32[165,2048]{1,0:T(8,128)}, f32[64,165]{1,0:T(8,128)}) custom-call(f32[165,2048]{1,0:T(8,128)} %mult_ref.1, f32[64,165]{1,0:T(8,128)} %bitcast.8, f32[165,32,165]{2,1,0:T(8,128)} %bitcast.7, s32[96,128]{1,0:T(8,128)} %pad_add_fusion.codes_ref, s32[8,16]{1,0:T(8,128)} %bitcast.9, s32[32,32]{1,0:T(8,128)} %lists_ref.1, s32[1]{0:T(128)S(6)} %copy.15.live_ref), custom_call_target="tpu_custom_call" | custom-call | flops 14273740800 | bytes 8388608 | tf_op jit(solution)/shard_map/far_field/pallas_call | solution.py:487
  140.0 0.0 copy-start
  140.0 2.6 %copy.16 = f32[165,2048]{1,0:T(8,128)} copy(f32[165,2048]{1,0:T(8,128)} %get-tuple-element.10) | data formatting | bytes 2703360
  142.6 0.0 copy-done
  142.6 0.6 copy.17
Async XLA Ops:
  140.0 2.6 %copy-start = (f32[64,165]{1,0:T(8,128)S(1)}, f32[64,165]{1,0:T(8,128)}, u32[]{:S(2)}) copy-start(f32[64,165]{1,0:T(8,128)} %get-tuple-element.5) | copy-start | bytes 126724

commit v4 on v3

--- a/solution.py
+++ b/solution.py
@@ -14,10 +14,11 @@
 PACKED = 24
 CHUNK = 4
 WIDE = 16
-STRIDE = 2
-OFFSETS = (0, 2, 4, 6, 9, 13, 15, 17, 19)
-X_TICK, Y_TICK, CORE_TICK, COARSE_TICK = 2, 5, 12, 20
-ARRANGE_TICK, ARRANGE_STEP = 4, 4
+STRIDES = (1, 1, 1, 1, 1, 1, 1, 1, 1)
+ORDER = (0, 1, 2, 3, 4, 5, 6, 7)
+OFFSETS = (0, 1, 2, 3, 4, 6, 7, 8, 9)
+X_TICK, Y_TICK, CORE_TICK, COARSE_TICK = 1, 5, 9, 11
+ARRANGE_TICK, ARRANGE_STEP = 2, 6
 MESH = pl.DeviceIdType.MESH
 
 
@@ -27,7 +28,7 @@
 
 def fine_kernel(
     groups, steps, own, sent, low_bits, offsets,
-    mult_ref, coarse_ref, ops_hbm, codes_ref, send_ref, lists_ref, live_ref,
+    mult_ref, coarse_ref, ops_hbm, codes_ref, send_ref, lists_ref,
     out_ref, coarse_out_ref,
     table, outgo, landed, split, mats, total, ops_ref,
     packed, everything, codes, codes_smem, replicas, gathered, partial, incoming,
@@ -114,22 +115,37 @@
         up = lax.rem(gx // bit, 2)
         return (gx + bit - 2 * bit * up, gy)
 
-    def copy(g, k):
+    def copy(g, k, count=sent):
         return pltpu.make_async_remote_copy(
-            src_ref=outgo.at[g, k],
-            dst_ref=landed.at[g, k],
+            src_ref=outgo.at[g, k, pl.ds(0, count)],
+            dst_ref=landed.at[g, k, pl.ds(0, count)],
             send_sem=send_sem.at[g, k],
             recv_sem=recv_sem.at[g, k],
             device_id=partner(k),
             device_id_type=MESH,
         )
+
+    def receive(g, k):
+        first = own + k * sent
+
+        @pl.when(g < groups - 1)
+        def _():
+            copy(g, k).wait_recv()
+            table[g, first : first + sent] = landed[g, k]
+
+        @pl.when(g == groups - 1)
+        def _():
+            copy(g, k, sent // 2).wait_recv()
+            for i in range(sent // 2):
+                both = landed[g, k, i]
+                table[g, first + i] = jnp.where(half, both, 0.0)
+                table[g, first + sent // 2 + i] = jnp.where(half, pltpu.roll(both, 64, 1), 0.0)
 
     barrier = pltpu.get_barrier_semaphore()
     peers = [x_device(o) for o in range(1, XCHIPS)] + [z_device(o) for o in range(1, 8)]
     peers += [y_device(o) for o in range(1, 4)] + [core_device()]
     for peer in peers:
         pl.semaphore_signal(barrier, inc=1, device_id=peer, device_id_type=MESH)
-    lax.fori_loop(0, slots, lambda j, c: (ops_copy(j).start(), c)[1], 0)
 
     lane64 = lax.broadcasted_iota(jnp.int32, (cells, 128), 1)
     near = coarse_ref[:, :128]
@@ -183,18 +199,35 @@
 
         lax.fori_loop(0, own // 2, pair, 0)
 
-    own_blocks(0)
     split[0] = jnp.zeros((ROWS, 128), jnp.bfloat16)
     pl.semaphore_wait(barrier, len(peers))
 
     def send(g, k):
+        if k == 0:
+
+            @pl.when(g < groups - 1)
+            def _():
+                own_blocks(g)
+
+            @pl.when(g == groups - 1)
+            def _():
+                last_blocks()
+
         if k > 0:
-            copy(g, k - 1).wait_recv()
-            first = own + (k - 1) * sent
-            table[g, first : first + sent] = landed[g, k - 1]
-        for i in range(sent):
-            outgo[g, k, i] = table[g, send_ref[k, i]]
-        copy(g, k).start()
+            receive(g, k - 1)
+
+        @pl.when(g < groups - 1)
+        def _():
+            for i in range(sent):
+                outgo[g, k, i] = table[g, send_ref[k, i]]
+            copy(g, k).start()
+
+        @pl.when(g == groups - 1)
+        def _():
+            for i in range(sent // 2):
+                other = pltpu.roll(table[g, send_ref[k, sent // 2 + i]], 64, 1)
+                outgo[g, k, i] = jnp.where(half, table[g, send_ref[k, i]], other)
+            copy(g, k, sent // 2).start()
 
     def arrange(n):
         q, at = n // groups, pl.multiple_of(lax.rem(n, groups) * ROWS, ROWS)
@@ -261,9 +294,6 @@
             )
 
     def multiply(g):
-        copy(g, steps - 1).wait_recv()
-        first = own + (steps - 1) * sent
-        table[g, first : first + sent] = landed[g, steps - 1]
         halves = lanes_below((16, 8, 128), 64)
 
         def cut(c, carry):
@@ -276,7 +306,10 @@
             split[pl.ds(at + 1, 16)] = jnp.concatenate([top, bottom], axis=1).astype(jnp.bfloat16)
             return carry
 
-        lax.fori_loop(0, (own + steps * sent) // 16, cut, 0, unroll=True)
+        known = (own + (steps - 1) * sent) // 16
+        lax.fori_loop(0, known, cut, 0, unroll=True)
+        receive(g, steps - 1)
+        lax.fori_loop(known, known + sent // 16, cut, 0)
         height = mats.shape[1] // 2
 
         def targets(p, carry):
@@ -339,10 +372,22 @@
     for o in range(1, XCHIPS):
         slice_copy(o).start()
         code_copy(o).start()
-    total[...] = jnp.zeros_like(total)
-    partial[...] = jnp.zeros_like(partial)
 
     def tick(s, carry):
+        for k in ORDER:
+            late = s - offsets[k]
+            g = late // STRIDES[k]
+
+            @pl.when((late >= 0) & (g < groups) & (lax.rem(late, STRIDES[k]) == 0))
+            def _():
+                send(g, k)
+
+        @pl.when(s == 0)
+        def _():
+            lax.fori_loop(0, slots, lambda j, c: (ops_copy(j).start(), c)[1], 0)
+            total[...] = jnp.zeros_like(total)
+            partial[...] = jnp.zeros_like(partial)
+
         @pl.when(s == X_TICK)
         def _():
             for o in range(1, XCHIPS):
@@ -366,24 +411,6 @@
                 code_copy(o).wait_recv()
             codes_copy().start()
 
-        for k in reversed(range(steps)):
-            late = s - offsets[k]
-            g = late // STRIDE
-
-            @pl.when((late >= 0) & (g < groups) & (lax.rem(late, STRIDE) == 0))
-            def _():
-                send(g, k)
-
-        g = s // STRIDE + 1
-
-        @pl.when((g < groups - 1) & (lax.rem(s, STRIDE) == 0))
-        def _():
-            own_blocks(g)
-
-        @pl.when((g == groups - 1) & (lax.rem(s, STRIDE) == 0))
-        def _():
-            last_blocks()
-
         @pl.when(s == ARRANGE_TICK)
         def _():
             lax.fori_loop(0, slots, lambda j, c: (ops_copy(j).wait(), c)[1], 0)
@@ -410,22 +437,24 @@
                 sum_copy(o).start()
 
         late = s - offsets[steps]
-        g = late // STRIDE
-
-        @pl.when((late >= 0) & (g < groups) & (lax.rem(late, STRIDE) == 0))
+        g = late // STRIDES[steps]
+
+        @pl.when((late >= 0) & (g < groups) & (lax.rem(late, STRIDES[steps]) == 0))
         def _():
             multiply(g)
 
         return carry
 
-    lax.fori_loop(0, (groups - 1) * STRIDE + offsets[steps] + 1, tick, 0)
+    lax.fori_loop(0, (groups - 1) * STRIDES[steps] + offsets[steps] + 1, tick, 0)
 
     def drain(g, carry):
         for k in range(steps):
             copy(g, k).wait_send()
         return carry
 
-    lax.fori_loop(0, groups, drain, 0)
+    lax.fori_loop(0, groups - 1, drain, 0)
+    for k in range(steps):
+        copy(groups - 1, k, sent // 2).wait_send()
 
     for o in range(1, XCHIPS):
         sum_copy(o).wait_recv()
@@ -441,7 +470,6 @@
         z_copy(o).wait_send()
     core_copy().wait_send()
 
-    live = live_ref[0]
     side = lanes_below((coef, 128), 64)
 
     def finish(p, carry):
@@ -450,11 +478,10 @@
         left = left + pltpu.roll(left, 64, 1)
         right = right + pltpu.roll(right, 64, 1)
         both = jnp.where(side, left, right)
-        position = 2 * p + jnp.where(side, 0, 1)
-        out_ref[:, pl.ds(pl.multiple_of(p * 128, 128), 128)] = jnp.where(position < live, both, 0.0)
+        out_ref[:, pl.ds(pl.multiple_of(p * 128, 128), 128)] = both
         return carry
 
-    lax.fori_loop(0, own // 2, finish, 0)
+    lax.fori_loop(0, own // 2, finish, 0, unroll=4)
 
 
 def source_codes(coarse_lists):
@@ -490,7 +517,7 @@
             jax.ShapeDtypeStruct((coef, cells), f32),
             jax.ShapeDtypeStruct((coarse_cells, coef), f32),
         ),
-        in_specs=[vmem, vmem, pl.BlockSpec(memory_space=pl.ANY), vmem, smem, smem, smem],
+        in_specs=[vmem, vmem, pl.BlockSpec(memory_space=pl.ANY), vmem, smem, smem],
         out_specs=(vmem, vmem),
         scratch_shapes=[
             pltpu.VMEM((groups, held, 8, 128), f32),
@@ -539,9 +566,9 @@
         source_codes(coarse_lists),
         send_lists[0],
         block_lists,
-        live_blocks,
     )
-    return (fine_local, coarse_local.T)
+    inside = jnp.arange(cells, dtype=jnp.int32) < live_blocks[0] * BCELLS
+    return (jnp.where(inside[None, :], fine_local, 0.0), coarse_local.T)
 
 
 def solution(mesh):

time: 143 us -> 134 us (0.937)
  Pallas kernels: 137 us -> 127 us
  other arithmetic: 0.79 us -> 3.39 us
  local copies, waits for them, and re-layouts: 4.08 us -> 1.5 us
    pallas_call x1, Pallas kernels: 137 us -> 127 us  [shards(): pl.pallas_call(functools.partial(fine_kernel, groups, steps, own, sent, l...]
    select_n x0 -> x1, other arithmetic: none -> 2.59 us  [shards(): return (jnp.where(inside[None, :], fine_local, 0.0), coarse_local.T)]
    unnamed x6 -> x5, local copies, waits for them, and re-layouts: 4.08 us -> 1.5 us
where the time goes in v4:
time: 134 us; the launch traced here: 133 us
  Pallas kernels  127 us (95%)
  other arithmetic  3.39 us (3%)
  local copies, waits for them, and re-layouts  1.5 us (1%)
    pallas_call x1, Pallas kernels, shards(): pl.pallas_call(functools.partial(fine_kernel, groups, steps, own, sent, l...  127 us

profile of v4, /device:TPU:8, one launch (start us, length us, event | category | flops | bytes accessed | tf_op | source)
XLA Modules:
  0.0 133.2 jit_solution(2226135618149711234)
XLA Ops:
  1.3 0.8 copy.9
  2.1 0.2 fusion.8
  2.2 0.1 copy.12
  2.3 0.6 pad_add_fusion.codes_ref
  3.0 127.0 %far_field.1 = (f32[165,2048]{1,0:T(8,128)}, f32[64,165]{1,0:T(8,128)}) custom-call(f32[165,2048]{1,0:T(8,128)} %mult_ref.1, f32[64,165]{1,0:T(8,128)} %bitcast.9, f32[165,32,165]{2,1,0:T(8,128)} %bitcast.8, s32[96,128]{1,0:T(8,128)} %pad_add_fusion.codes_ref, s32[8,16]{1,0:T(8,128)} %bitcast.10, s32[32,32]{1,0:T(8,128)} %lists_ref.1), custom_call_target="tpu_custom_call" | custom-call | flops 14273740800 | bytes 8388608 | tf_op jit(solution)/shard_map/far_field/pallas_call | solution.py:514
  130.0 0.0 copy-start
  130.0 2.6 %broadcast_select_fusion = f32[165,2048]{1,0:T(8,128)} fusion(f32[165,2048]{1,0:T(8,128)} %get-tuple-element.4, pred[2048]{0:T(1024)(128)(4,1)S(1)} %iota_compare_fusion), kind=kLoop, calls=%fused_computation | loop fusion | flops 337920 | bytes 2705408 | tf_op jit(solution)/shard_map/jit(_where)/select_n | solution.py:571
  132.6 0.0 copy-done
  132.6 0.6 copy.15
  (1 shorter events, 0.0 us)
Async XLA Ops:
  130.0 2.6 %copy-start = (f32[64,165]{1,0:T(8,128)S(1)}, f32[64,165]{1,0:T(8,128)}, u32[]{:S(2)}) copy-start(f32[64,165]{1,0:T(8,128)} %get-tuple-element.5) | copy-start | bytes 126724

commit v5 on v4

--- a/solution.py
+++ b/solution.py
@@ -13,7 +13,7 @@
 PARTS = 3
 PACKED = 24
 CHUNK = 4
-WIDE = 16
+WIDE = 32
 STRIDES = (1, 1, 1, 1, 1, 1, 1, 1, 1)
 ORDER = (0, 1, 2, 3, 4, 5, 6, 7)
 OFFSETS = (0, 1, 2, 3, 4, 6, 7, 8, 9)

time: 134 us -> 133 us (level)
  no operation moved by 1% of the time
where the time goes in v5:
time: 133 us
  Pallas kernels  126 us (95%)
  other arithmetic  3.39 us (3%)
  local copies, waits for them, and re-layouts  1.5 us (1%)
    pallas_call x1, Pallas kernels, shards(): pl.pallas_call(functools.partial(fine_kernel, groups, steps, own, sent, l...  126 us

profile of v5, /device:TPU:8, one launch (start us, length us, event | category | flops | bytes accessed | tf_op | source)
XLA Modules:
  0.0 132.5 jit_solution(12538883164198152347)
XLA Ops:
  1.3 0.8 copy.9
  2.1 0.2 fusion.8
  2.2 0.1 copy.12
  2.3 0.6 pad_add_fusion.codes_ref
  3.0 126.3 %far_field.1 = (f32[165,2048]{1,0:T(8,128)}, f32[64,165]{1,0:T(8,128)}) custom-call(f32[165,2048]{1,0:T(8,128)} %mult_ref.1, f32[64,165]{1,0:T(8,128)} %bitcast.9, f32[165,32,165]{2,1,0:T(8,128)} %bitcast.8, s32[96,128]{1,0:T(8,128)} %pad_add_fusion.codes_ref, s32[8,16]{1,0:T(8,128)} %bitcast.10, s32[32,32]{1,0:T(8,128)} %lists_ref.1), custom_call_target="tpu_custom_call" | custom-call | flops 14273740800 | bytes 8388608 | tf_op jit(solution)/shard_map/far_field/pallas_call | solution.py:514
  129.3 0.0 copy-start
  129.3 2.6 %broadcast_select_fusion = f32[165,2048]{1,0:T(8,128)} fusion(f32[165,2048]{1,0:T(8,128)} %get-tuple-element.4, pred[2048]{0:T(1024)(128)(4,1)S(1)} %iota_compare_fusion), kind=kLoop, calls=%fused_computation | loop fusion | flops 337920 | bytes 2705408 | tf_op jit(solution)/shard_map/jit(_where)/select_n | solution.py:571
  131.9 0.0 copy-done
  131.9 0.6 copy.15
  (1 shorter events, 0.0 us)
Async XLA Ops:
  129.3 2.6 %copy-start = (f32[64,165]{1,0:T(8,128)S(1)}, f32[64,165]{1,0:T(8,128)}, u32[]{:S(2)}) copy-start(f32[64,165]{1,0:T(8,128)} %get-tuple-element.5) | copy-start | bytes 126724
